TPU v7x, 32 devices: a whole 2x2x4 slice. The times are simulated.
32 devices in a mesh: parts: 2 (over y), rows: 4 (over z), cols: 2 (over x), sub: 2 (over core).
Axes of the slice: x: 2, y: 2, z: 4, core: 2. Of those that a mesh axis runs over, the one named last changes fastest.
Arguments:
- left_states: float32 [32, 2, 65536], P(('parts', 'rows', 'cols', 'sub')), parts along dimension 0, may hold values from -6 to 6
- right_states: float32 [32, 2, 65536], P(('parts', 'rows', 'cols', 'sub')), parts along dimension 0, may hold values from -6 to 6
- gates: float32 [4, 2, 128, 128], P('parts'), parts along dimension 0, may hold values from -0.375 to 0.375
- left_index: int32 [2048], P('parts'), parts along dimension 0, may hold values from 0 to 65535
- right_index: int32 [2048], P('parts'), parts along dimension 0, may hold values from 0 to 65535
Outputs:
- amplitudes: float32 [4, 1024, 1024], P('parts', 'rows', ('cols', 'sub')), parts along dimension 0
There are 2 independent parts, one for each index of `parts`. A program takes and returns all parts, laid end to end along the dimension named above; each array names one. Nothing has to cross between parts.
All inputs are finite; a program needn't handle non-finite values.
Results may differ from a plain program's by a relative error of at most 0.000073.
Values sent between devices are 32-bit elements; how exact they have to be, the bound alone decides.
A program may use at most 64 MiB of HBM per device.

v0:
```python
import jax
import jax.numpy as jnp
from jax import lax
from jax.sharding import PartitionSpec as P

GATE = 128


def apply_layers(states, gates):
    highest = lax.Precision.HIGHEST
    count = states.shape[0]
    real = states[:, 0].reshape(count, -1, GATE)
    imag = states[:, 1].reshape(count, -1, GATE)
    u_real, u_imag = (gates[0, 0], gates[0, 1])
    new_real = jnp.einsum("nag,hg->nah", real, u_real, precision=highest) - jnp.einsum(
        "nag,hg->nah", imag, u_imag, precision=highest
    )
    new_imag = jnp.einsum("nag,hg->nah", real, u_imag, precision=highest) + jnp.einsum(
        "nag,hg->nah", imag, u_real, precision=highest
    )
    real = new_real.reshape(count, -1, GATE, GATE)
    imag = new_imag.reshape(count, -1, GATE, GATE)
    v_real, v_imag = (gates[1, 0], gates[1, 1])
    out_real = jnp.einsum("qm,nhml->nhql", v_real, real, precision=highest) - jnp.einsum(
        "qm,nhml->nhql", v_imag, imag, precision=highest
    )
    out_imag = jnp.einsum("qm,nhml->nhql", v_imag, real, precision=highest) + jnp.einsum(
        "qm,nhml->nhql", v_real, imag, precision=highest
    )
    return (out_real.reshape(count, -1), out_imag.reshape(count, -1))


def pick_values(states, gates, index):
    real, imag = apply_layers(states, gates)
    return jnp.stack([jnp.take(real, index, axis=1), jnp.take(imag, index, axis=1)])


def transposed_product(first, second):
    return lax.dot_general(
        first,
        second,
        (((0,), (0,)), ((), ())),
        precision=lax.Precision.HIGHEST,
        preferred_element_type=jnp.float32,
    )


def per_device(left_states, right_states, gates, left_index, right_index):
    left_pick = pick_values(left_states, gates, left_index)
    right_pick = pick_values(right_states, gates, right_index)
    held = left_pick.shape[1]
    nleft = left_pick.shape[2]
    nright = right_pick.shape[2]
    row_count = lax.axis_size("rows")
    group = lax.axis_size("cols") * lax.axis_size("sub")
    tile_rows = nleft // row_count
    tile_cols = nright // group
    moved = lax.all_to_all(
        left_pick.reshape(2, 1, held, nleft), "rows", split_axis=3, concat_axis=1, tiled=True
    )
    moved = lax.all_gather(
        moved.reshape(2, row_count, 1, held, tile_rows), ("cols", "sub"), axis=2, tiled=True
    )
    left_all = moved.reshape(2, -1, tile_rows)
    spread = lax.all_to_all(
        right_pick.reshape(2, 1, held, nright),
        ("cols", "sub"),
        split_axis=3,
        concat_axis=1,
        tiled=True,
    )
    flat = lax.all_gather(
        spread.reshape(2, 1, group, held, tile_cols), "rows", axis=1, tiled=True
    ).reshape(2, -1, tile_cols)
    out_real = transposed_product(left_all[0], flat[0]) - transposed_product(left_all[1], flat[1])
    out_imag = transposed_product(left_all[0], flat[1]) + transposed_product(left_all[1], flat[0])
    total = jnp.stack([out_real, out_imag])
    scale = jnp.float32(1.0) / jnp.sqrt(jnp.float32(left_all.shape[1]))
    return total * scale


def solution(mesh):
    return jax.shard_map(
        per_device,
        mesh=mesh,
        in_specs=(
            P(("parts", "rows", "cols", "sub"), None, None),
            P(("parts", "rows", "cols", "sub"), None, None),
            P("parts", None, None, None),
            P("parts"),
            P("parts"),
        ),
        out_specs=P("parts", "rows", ("cols", "sub")),
        check_vma=False,
    )
```

profile of v0, /device:TPU:0, one launch (start us, length us, event | category | flops | bytes accessed | tf_op | source)
XLA Modules:
  0.0 77.1 jit_solution(12147465067871130545)
XLA Ops:
  0.0 1.7 %fusion.50 = (f32[1,1,65536]{2,1,0:T(1,128)S(1)}, f32[1,1,65536]{2,1,0:T(1,128)S(1)}) fusion(f32[1,2,65536]{2,1,0:T(2,128)} %param.8), kind=kLoop, calls=%fused_computation.81 | loop fusion | bytes 1048576 | tf_op jit(solution)/shard_map/slice | solution.py:13
  2.9 0.6 fusion.14
  3.5 0.6 fusion.9
  4.6 0.6 fusion.1
  5.2 0.6 fusion
  6.0 6.2 %gather_fusion.3 = f32[1024]{0:T(1024)S(1)} fusion(f32[65536]{0:T(1024)S(1)} %bitcast.152, s32[1024]{0:T(1024)S(1)} %fusion.49), kind=kCustom, calls=%fused_computation.3.clone | custom fusion | bytes 12288 | tf_op jit(solution)/shard_map/jit(_take)/gather | solution.py:35
  12.2 6.2 %gather_fusion.2 = f32[1024]{0:T(1024)S(1)} fusion(f32[65536]{0:T(1024)S(1)} %bitcast.150, s32[1024]{0:T(1024)S(1)} %fusion.49), kind=kCustom, calls=%fused_computation.2.clone | custom fusion | bytes 12288 | tf_op jit(solution)/shard_map/jit(_take)/gather | solution.py:35
  19.3 1.9 %reduce.2 = f32[1024,2]{1,0:T(8,128)S(1)} reduce(f32[1024,1,1,2]{3,2,1,0:T(1,128)S(1)} %bitcast.170, f32[]{:T(128)} %broadcast.17), dimensions={1,2}, to_apply=%bitcast.132.reduce_sub_computation | reduce | bytes 16388
  21.3 0.9 %reshape.238 = f32[4,1,512]{2,1,0:T(1,128)} reshape(f32[1024,2]{1,0:T(8,128)S(1)} %reduce.2) | data formatting | bytes 16384
  22.2 4.2 %all-to-all-start.1 = ((f32[4,1,512]{2,1,0:T(1,128)}), f32[4,1,512]{2,1,0:T(1,128)S(1)}, u32[]{:S(2)}, u32[]{:S(2)}) async-start(f32[4,1,512]{2,1,0:T(1,128)} %reshape.238), calls=%async_computation.1 | async-start | bytes 16384 | tf_op jit(solution)/shard_map/all_to_all | solution.py:65
  29.6 0.6 fusion.3
  30.2 0.6 fusion.2
  31.1 6.2 %gather_fusion.1 = f32[1024]{0:T(1024)S(1)} fusion(f32[65536]{0:T(1024)S(1)} %bitcast.153, s32[1024]{0:T(1024)S(1)} %fusion.48), kind=kCustom, calls=%fused_computation.1.clone | custom fusion | bytes 12288 | tf_op jit(solution)/shard_map/jit(_take)/gather | solution.py:35
  37.3 6.2 %gather_fusion = f32[1024]{0:T(1024)S(1)} fusion(f32[65536]{0:T(1024)S(1)} %bitcast.151, s32[1024]{0:T(1024)S(1)} %fusion.48), kind=kCustom, calls=%fused_computation.clone | custom fusion | bytes 12288 | tf_op jit(solution)/shard_map/jit(_take)/gather | solution.py:35
  43.8 1.9 %reduce = f32[1024,2]{1,0:T(8,128)S(1)} reduce(f32[1024,1,1,2]{3,2,1,0:T(1,128)S(1)} %bitcast.171, f32[]{:T(128)} %broadcast.17), dimensions={1,2}, to_apply=%bitcast.130.reduce_sub_computation | reduce | bytes 16388
  45.8 0.9 %reshape.236 = f32[4,1,512]{2,1,0:T(1,128)} reshape(f32[1024,2]{1,0:T(8,128)S(1)} %reduce) | data formatting | bytes 16384
  46.7 5.5 %all-to-all-start = ((f32[4,1,512]{2,1,0:T(1,128)}), f32[4,1,512]{2,1,0:T(1,128)S(1)}, u32[]{:S(2)}, u32[]{:S(2)}) async-start(f32[4,1,512]{2,1,0:T(1,128)} %reshape.236), calls=%async_computation | async-start | bytes 16384 | tf_op jit(solution)/shard_map/all_to_all | solution.py:58
  52.2 0.7 reduce.3
  52.9 0.9 %reshape.239 = f32[1024,1,1,2]{3,2,1,0:T(1,128)S(1)} reshape(f32[4,512]{1,0:T(4,128)S(1)} %reduce.3) | data formatting | bytes 16384
  53.9 13.7 %all_gather.7 = f32[2,4,4,1,256]{4,2,1,3,0:T(4,128)S(1)} all-gather(f32[2,1,4,1,256]{4,2,1,3,0:T(4,128)S(1)} %copy.68), channel_id=1, replica_groups=mesh['parts'=2,'rows'=4,'cols'=2,'sub'=2] {'rows'}, dimensions={1}, use_global_device_ids=true | all-gather | bytes 40960 | tf_op jit(solution)/shard_map/all_gather | solution.py:72
  67.6 0.7 reduce.1
  68.3 0.9 %reshape.237 = f32[1024,1,1,2]{3,2,1,0:T(1,128)S(1)} reshape(f32[4,512]{1,0:T(4,128)S(1)} %reduce.1) | data formatting | bytes 16384
  69.4 5.2 %all_gather.6 = f32[2,4,4,1,256]{4,1,3,0,2:T(4,128)S(1)} all-gather(f32[2,4,1,1,256]{4,1,3,0,2:T(4,128)S(1)} %copy.49), channel_id=1, replica_groups=mesh['parts'=2,'rows'=4,'cols'=2,'sub'=2] {'cols','sub'}, dimensions={2}, use_global_device_ids=true | all-gather | bytes 40960 | tf_op jit(solution)/shard_map/all_gather | solution.py:61
  76.3 0.8 %maximum_multiply_fusion = f32[2,256,256]{2,1,0:T(8,128)} fusion(f32[1,256,256]{2,1,0:T(8,128)S(1)} %fusion.7, f32[1,256,256]{2,1,0:T(8,128)S(1)} %fusion.5), kind=kLoop, calls=%fused_computation.24 | loop fusion | flops 262144 | bytes 1048576 | tf_op jit(solution)/shard_map/mul | solution.py:79
  (43 shorter events, 8.7 us)
Async XLA Ops:
  0.0 1.7 %copy-start = (f32[2,2,128,128]{3,2,1,0:T(8,128)S(1)}, f32[2,2,128,128]{3,2,1,0:T(8,128)}, u32[]{:S(2)}) copy-start(f32[2,2,128,128]{3,2,1,0:T(8,128)} %param.9) | copy-start | bytes 786436
  3.5 0.7 copy-start.2
  21.3 5.1 %copy-start.1 = (f32[1,2,65536]{2,1,0:T(2,128)S(1)}, f32[1,2,65536]{2,1,0:T(2,128)}, u32[]{:S(2)}) copy-start(f32[1,2,65536]{2,1,0:T(2,128)} %param.7) | copy-start | bytes 1572868
  22.2 24.5 %all-to-all-start.1 = ((f32[4,1,512]{2,1,0:T(1,128)}), f32[4,1,512]{2,1,0:T(1,128)S(1)}, u32[]{:S(2)}, u32[]{:S(2)}) async-start(f32[4,1,512]{2,1,0:T(1,128)} %reshape.238), calls=%async_computation.1 | async-start | bytes 16384 | tf_op jit(solution)/shard_map/all_to_all | solution.py:65
  28.6 0.7 copy-start.3
  46.7 20.9 %all-to-all-start = ((f32[4,1,512]{2,1,0:T(1,128)}), f32[4,1,512]{2,1,0:T(1,128)S(1)}, u32[]{:S(2)}, u32[]{:S(2)}) async-start(f32[4,1,512]{2,1,0:T(1,128)} %reshape.236), calls=%async_computation | async-start | bytes 16384 | tf_op jit(solution)/shard_map/all_to_all | solution.py:58
where the time goes:
time: 77.5 us; the launch traced here: 77.1 us
  local copies, waits for them, and re-layouts  32.6 us (42%)
  blocking collectives  18.9 us (24%)
  starting transfers between devices  9.74 us (13%)
  matrix products  9.48 us (12%)
  other arithmetic  6.07 us (8%)
    all_gather x1, blocking collectives, per_device(): lax.all_gather(spread.reshape(2, 1, group, held, tile_cols), 'rows', axis...  13.7 us
    gather x2, local copies, waits for them, and re-layouts, pick_values(): jnp.take(imag, index, axis=1)  12.3 us
    gather x2, local copies, waits for them, and re-layouts, pick_values(): jnp.take(real, index, axis=1)  12.3 us
    all_to_all x1, starting transfers between devices, per_device(): lax.all_to_all(left_pick.reshape(2, 1, held, nleft), 'rows', split_axis=3...  5.53 us
    all_gather x1, blocking collectives, per_device(): lax.all_gather(moved.reshape(2, row_count, 1, held, tile_rows), ('cols',...  5.19 us
    unnamed x13, local copies, waits for them, and re-layouts  4.32 us
    all_to_all x1, starting transfers between devices, per_device(): lax.all_to_all(right_pick.reshape(2, 1, held, nright), ('cols', 'sub'), s...  4.21 us
    unnamed x2, other arithmetic  3.86 us
  transfers between devices with their start and end apart: 2, of which 0 were waited for; matrix products, arithmetic and copies ran while one was open for 28% of the time, Pallas kernels for 0%

commit v1 on v0

v1 whole, which is shorter than its diff:
```python
import functools
import math

import jax
import jax.numpy as jnp
from jax import lax
from jax.experimental import pallas as pl
from jax.experimental.pallas import tpu as pltpu
from jax.sharding import PartitionSpec as P

MESH = pl.DeviceIdType.MESH
BF16 = jnp.bfloat16
F32 = jnp.float32


def split(x):
    high = x.astype(BF16)
    return high, (x - high.astype(F32)).astype(BF16)


def dot(a, b, dims=((1,), (0,))):
    return lax.dot_general(a, b, (dims, ((), ())), preferred_element_type=F32)


def for_blocks(count, body):
    if count <= 4:
        for b in range(count):
            body(b)
    else:

        def step(b, carry):
            body(b)
            return carry

        lax.fori_loop(0, count, step, 0)


def half_picks(state_ref, p, gate, second, index_ref, width, picked_ref, emit):
    size = gate[0].shape[0] // 2
    rows = state_ref.shape[1] // 2
    slabs = rows // size
    real = state_ref[p, pl.ds(0, rows, stride=2), :]
    imag = state_ref[p, pl.ds(1, rows, stride=2), :]
    xh, xl = split(jnp.concatenate([real, imag], axis=1))
    gh, gl = gate
    nt = ((1,), (1,))
    first = dot(xh, gh, nt) + (dot(xl, gh, nt) + dot(xh, gl, nt))
    parts = [
        jnp.concatenate(
            [first[h * size : (h + 1) * size, c * size : (c + 1) * size] for h in range(slabs)], axis=1
        )
        for c in range(2)
    ]
    high, low = split(jnp.concatenate(parts, axis=0))
    picked_ref[: 2 * size, :] = high
    picked_ref[2 * size :, :] = low

    def body(b):
        at = b * width if isinstance(b, int) else pl.multiple_of(b * width, width)
        index = index_ref[:, pl.ds(at, width)]
        low_bits = lax.rem(index, size)
        mid = lax.rem(lax.div(index, size), size)
        column = lax.div(index, size * size) * size + low_bits
        spot = lax.broadcasted_iota(jnp.int32, (slabs * size, width), 0)
        hot = jnp.where(spot == column, 1.0, 0.0).astype(BF16)
        found = dot(picked_ref[...], hot)
        found = found[: 2 * size] + found[2 * size :]
        spot = lax.broadcasted_iota(jnp.int32, (size, width), 0)
        hot = jnp.where(spot == mid, 1.0, 0.0).astype(BF16)
        rows2 = dot(second, jnp.concatenate([hot, hot], axis=0))
        fr, fi = found[:size], found[size:]
        vr, vi = rows2[:size], rows2[size:]
        out_r = jnp.sum(vr * fr - vi * fi, axis=0, keepdims=True)
        out_i = jnp.sum(vr * fi + vi * fr, axis=0, keepdims=True)
        lanes = width // 128
        emit(
            b,
            jnp.concatenate(
                [o[:, k * 128 : (k + 1) * 128] for o in (out_r, out_i) for k in range(lanes)], axis=0
            ),
        )

    for_blocks(index_ref.shape[1] // width, body)


def kernel(
    counts,
    left_ref,
    right_ref,
    gates_ref,
    left_index_ref,
    right_index_ref,
    out_ref,
    left_buf,
    right_buf,
    picked,
    send,
    recv,
    load_sem,
    send_sem,
    recv_sem,
):
    row_count, col_count, sub_count = counts
    group = col_count * sub_count
    n = row_count * group
    held = left_buf.shape[0]
    tile_l = left_index_ref.shape[1] // row_count
    tile_r = right_index_ref.shape[1] // group
    rows_l = 2 * tile_l // 128
    rows_r = 2 * tile_r // 128
    unit = rows_l + rows_r
    slot = held * unit
    me = (lax.axis_index("rows") * col_count + lax.axis_index("cols")) * sub_count + lax.axis_index("sub")

    load_l = pltpu.make_async_copy(left_ref, left_buf, load_sem.at[0])
    load_r = pltpu.make_async_copy(right_ref, right_buf, load_sem.at[1])
    load_l.start()
    load_r.start()

    def peer(offset):
        d = lax.rem(me + offset, n)
        where = {
            "rows": lax.div(d, group),
            "cols": lax.rem(lax.div(d, sub_count), col_count),
            "sub": lax.rem(d, sub_count),
        }
        return d, where

    barrier = pltpu.get_barrier_semaphore()

    def greet(offset, carry):
        pl.semaphore_signal(barrier, inc=1, device_id=peer(offset)[1], device_id_type=MESH)
        return carry

    lax.fori_loop(1, n, greet, 0)

    ur, ui = gates_ref[0, 0], gates_ref[0, 1]
    gate = split(
        jnp.concatenate(
            [jnp.concatenate([ur, -ui], axis=1), jnp.concatenate([ui, ur], axis=1)], axis=0
        )
    )
    second = jnp.concatenate(
        split(jnp.concatenate([gates_ref[1, 0].T, gates_ref[1, 1].T], axis=0)), axis=1
    )
    scale = 1.0 / math.sqrt(n * held)

    load_l.wait()
    for p in range(held):

        def emit_left(b, rows, p=p):
            rows = rows * scale
            for g in range(group):
                send[b * group + g, p * unit : p * unit + rows_l, :] = rows

        half_picks(left_buf, p, gate, second, left_index_ref, tile_l, picked, emit_left)
    load_r.wait()
    for p in range(held):

        def emit_right(b, rows, p=p):
            for r in range(row_count):
                send[r * group + b, p * unit + rows_l : (p + 1) * unit, :] = rows

        half_picks(right_buf, p, gate, second, right_index_ref, tile_r, picked, emit_right)

    pl.semaphore_wait(barrier, n - 1)

    def place(d):
        return recv.at[pl.ds(pl.multiple_of(d * slot, slot), slot), :]

    def push(offset, carry):
        d, where = peer(offset)
        pltpu.make_async_remote_copy(
            src_ref=send.at[d],
            dst_ref=place(me),
            send_sem=send_sem,
            recv_sem=recv_sem,
            device_id=where,
            device_id_type=MESH,
        ).start()
        return carry

    lax.fori_loop(1, n, push, 0)
    recv[pl.ds(pl.multiple_of(me * slot, slot), slot), :] = send[me]
    everything = recv.at[pl.ds(0, (n - 1) * slot), :]
    pltpu.make_async_copy(everything, everything, recv_sem).wait()

    def take(start, rows):
        return jnp.concatenate(
            [recv[pl.ds(start + t, n * held, stride=unit), :] for t in range(rows)], axis=1
        )

    lr, li = take(0, rows_l // 2), take(rows_l // 2, rows_l // 2)
    rr, ri = take(rows_l, rows_r // 2), take(rows_l + rows_r // 2, rows_r // 2)
    lh, ll = split(jnp.concatenate([lr, li], axis=0))
    rh, rl = split(
        jnp.concatenate(
            [jnp.concatenate([rr, -ri], axis=0), jnp.concatenate([ri, rr], axis=0)], axis=1
        )
    )
    left = jnp.concatenate([lh, lh, ll], axis=0)
    right = jnp.concatenate([rh, rl, rh], axis=0)
    result = dot(left, right, ((0,), (0,)))
    out_ref[0] = result[:, :tile_r]
    out_ref[1] = result[:, tile_r:]
    sent = send.at[pl.ds(0, n - 1)]
    pltpu.make_async_copy(sent, sent, send_sem).wait()


def per_device(counts, left_states, right_states, gates, left_index, right_index):
    row_count, col_count, sub_count = counts
    group = col_count * sub_count
    n = row_count * group
    size = gates.shape[-1]
    held = left_states.shape[0]
    nleft, nright = left_index.shape[0], right_index.shape[0]
    tile_l, tile_r = nleft // row_count, nright // group
    unit = 2 * (tile_l + tile_r) // 128
    slab = left_states.shape[2]

    def rows_of(states):
        return states.reshape(held, 2, slab // size, size).transpose(0, 2, 1, 3).reshape(held, -1, size)

    vmem = pl.BlockSpec(memory_space=pltpu.VMEM)
    hbm = pl.BlockSpec(memory_space=pl.ANY)
    return pl.pallas_call(
        functools.partial(kernel, counts),
        out_shape=jax.ShapeDtypeStruct((2, tile_l, tile_r), F32),
        in_specs=[hbm, hbm, vmem, vmem, vmem],
        out_specs=vmem,
        scratch_shapes=[
            pltpu.VMEM((held, 2 * slab // size, size), F32),
            pltpu.VMEM((held, 2 * slab // size, size), F32),
            pltpu.VMEM((4 * size, slab // size), BF16),
            pltpu.VMEM((n, held * unit, 128), F32),
            pltpu.VMEM((n * held * unit, 128), F32),
            pltpu.SemaphoreType.DMA((2,)),
            pltpu.SemaphoreType.DMA,
            pltpu.SemaphoreType.DMA,
        ],
        compiler_params=pltpu.CompilerParams(
            collective_id=0, has_side_effects=True, vmem_limit_bytes=40 * 1024 * 1024
        ),
    )(
        rows_of(left_states),
        rows_of(right_states),
        gates,
        left_index.reshape(1, nleft),
        right_index.reshape(1, nright),
    )


def solution(mesh):
    counts = tuple(mesh.shape[a] for a in ("rows", "cols", "sub"))
    return jax.shard_map(
        functools.partial(per_device, counts),
        mesh=mesh,
        in_specs=(
            P(("parts", "rows", "cols", "sub"), None, None),
            P(("parts", "rows", "cols", "sub"), None, None),
            P("parts", None, None, None),
            P("parts"),
            P("parts"),
        ),
        out_specs=P("parts", "rows", ("cols", "sub")),
        check_vma=False,
    )
```

time: 77.5 us -> 17 us (0.22)
  local copies, waits for them, and re-layouts: 32.6 us -> 5.2 us
  blocking collectives: 18.9 us -> 0 us
  Pallas kernels: 0 us -> 11.4 us
  starting transfers between devices: 9.74 us -> 0 us
  matrix products: 9.48 us -> 0 us
  other arithmetic: 6.07 us -> 0 us
    gather x4 -> x0, local copies, waits for them, and re-layouts: 24.6 us -> none  [the longest x2 12.3 us: pick_values(): jnp.take(imag, index, axis=1)]
    all_gather x2 -> x0, blocking collectives: 18.9 us -> none  [the longest x1 13.7 us: per_device(): lax.all_gather(spread.reshape(2, 1, group, held, tile_cols), 'rows', axis...]
    pallas_call x0 -> x1, Pallas kernels: none -> 11.4 us  [per_device(): pl.pallas_call(functools.partial(kernel, counts), out_shape=jax.ShapeDtyp...]
    all_to_all x2 -> x0, starting transfers between devices: 9.74 us -> none  [the longest x1 5.53 us: per_device(): lax.all_to_all(left_pick.reshape(2, 1, held, nleft), 'rows', split_axis=3...]
    dot_general x20 -> x0, matrix products: 9.48 us -> none  [the longest x4 1.71 us: transposed_product(): lax.dot_general(first, second, (((0,), (0,)), ((), ())), precision=lax.Pr...]
    unnamed x2 -> x0, other arithmetic: 3.86 us -> none
    slice x3 -> x0, local copies, waits for them, and re-layouts: 2.1 us -> none  [the longest x2 2.1 us: apply_layers(): imag = states[:, 1].reshape(count, -1, GATE)]
    all_to_all x2 -> x0, other arithmetic: 1.32 us -> none  [the longest x1 0.66 us: per_device(): lax.all_to_all(left_pick.reshape(2, 1, held, nleft), 'rows', split_axis=3...]
  transfers between devices with their start and end apart: 2 -> 0, of which waited for: 0 -> 0; matrix products, arithmetic and copies ran while one was open for 28% -> 0% of each run, Pallas kernels for 0% -> 0%
where the time goes in v1:
time: 17 us; the launch traced here: 16.7 us
  Pallas kernels  11.4 us (67%)
  local copies, waits for them, and re-layouts  5.2 us (31%)
    pallas_call x1, Pallas kernels, per_device(): pl.pallas_call(functools.partial(kernel, counts), out_shape=jax.ShapeDtyp...  11.4 us
    unnamed x11, local copies, waits for them, and re-layouts  5.2 us

profile of v1, /device:TPU:0, one launch (start us, length us, event | category | flops | bytes accessed | tf_op | source)
XLA Modules:
  0.0 16.7 jit_solution(17116267276932040473)
XLA Ops:
  0.0 0.0 copy-start.3
  0.0 0.7 %copy-done.3 = s32[1024]{0:T(1024)S(1)} copy-done((s32[1024]{0:T(1024)S(1)}, s32[1024]{0:T(1024)}, u32[]{:S(2)}) %copy-start.3) | copy-done | bytes 4120
  0.7 0.0 copy-start
  0.7 1.0 %copy-done = f32[1,2,65536]{2,1,0:T(2,128)S(1)} copy-done((f32[1,2,65536]{2,1,0:T(2,128)S(1)}, f32[1,2,65536]{2,1,0:T(2,128)}, u32[]{:S(2)}) %copy-start) | copy-done | bytes 524312
  1.7 0.0 copy-start.1
  1.7 1.0 %copy-done.1 = f32[1,2,65536]{2,1,0:T(2,128)S(1)} copy-done((f32[1,2,65536]{2,1,0:T(2,128)S(1)}, f32[1,2,65536]{2,1,0:T(2,128)}, u32[]{:S(2)}) %copy-start.1) | copy-done | bytes 524312
  2.8 0.0 copy-start.2
  2.8 0.9 %copy-done.2 = f32[2,2,128,128]{3,2,1,0:T(8,128)S(1)} copy-done((f32[2,2,128,128]{3,2,1,0:T(8,128)S(1)}, f32[2,2,128,128]{3,2,1,0:T(8,128)}, u32[]{:S(2)}) %copy-start.2) | copy-done | bytes 262168
  3.7 0.0 copy-start.4
  3.7 0.7 %copy-done.4 = s32[1024]{0:T(1024)S(1)} copy-done((s32[1024]{0:T(1024)S(1)}, s32[1024]{0:T(1024)}, u32[]{:S(2)}) %copy-start.4) | copy-done | bytes 4120
  4.4 11.4 %shard_map.55 = f32[2,256,256]{2,1,0:T(8,128)S(1)} custom-call(f32[1,1024,128]{2,1,0:T(8,128)S(1)} %bitcast.12, f32[1,1024,128]{2,1,0:T(8,128)S(1)} %bitcast.13, f32[2,2,128,128]{3,2,1,0:T(8,128)S(1)} %copy-done.2, s32[1,1024]{1,0:T(1,128)S(1)} %bitcast.14, s32[1,1024]{1,0:T(1,128)S(1)} %bitcast.15), custom_call_target="tpu_custom_call" | custom-call | tf_op jit(solution)/shard_map/pallas_call | solution.py:226
  15.9 0.8 %copy.9 = f32[2,256,256]{2,1,0:T(8,128)} copy(f32[2,256,256]{2,1,0:T(8,128)S(1)} %shard_map.55) | data formatting | bytes 1048576
Async XLA Ops:
  0.0 0.7 %copy-start.3 = (s32[1024]{0:T(1024)S(1)}, s32[1024]{0:T(1024)}, u32[]{:S(2)}) copy-start(s32[1024]{0:T(1024)} %param.8) | copy-start | bytes 12292
  0.7 1.0 %copy-start = (f32[1,2,65536]{2,1,0:T(2,128)S(1)}, f32[1,2,65536]{2,1,0:T(2,128)}, u32[]{:S(2)}) copy-start(f32[1,2,65536]{2,1,0:T(2,128)} %param.5) | copy-start | bytes 1572868
  1.7 1.0 %copy-start.1 = (f32[1,2,65536]{2,1,0:T(2,128)S(1)}, f32[1,2,65536]{2,1,0:T(2,128)}, u32[]{:S(2)}) copy-start(f32[1,2,65536]{2,1,0:T(2,128)} %param.6) | copy-start | bytes 1572868
  2.8 0.9 %copy-start.2 = (f32[2,2,128,128]{3,2,1,0:T(8,128)S(1)}, f32[2,2,128,128]{3,2,1,0:T(8,128)}, u32[]{:S(2)}) copy-start(f32[2,2,128,128]{3,2,1,0:T(8,128)} %gates_ref.1) | copy-start | bytes 786436
  3.7 0.7 %copy-start.4 = (s32[1024]{0:T(1024)S(1)}, s32[1024]{0:T(1024)}, u32[]{:S(2)}) copy-start(s32[1024]{0:T(1024)} %param.9) | copy-start | bytes 12292

commit v2 on v1

v2 whole, which is shorter than its diff:
```python
import functools
import math

import jax
import jax.numpy as jnp
from jax import lax
from jax.experimental import pallas as pl
from jax.experimental.pallas import tpu as pltpu
from jax.sharding import PartitionSpec as P

MESH = pl.DeviceIdType.MESH
BF16 = jnp.bfloat16
F32 = jnp.float32


def split(x):
    high = x.astype(BF16)
    return high, (x - high.astype(F32)).astype(BF16)


def dot(a, b, dims=((1,), (0,))):
    return lax.dot_general(a, b, (dims, ((), ())), preferred_element_type=F32)


def for_blocks(count, body):
    if count <= 4:
        for b in range(count):
            body(b)
    else:

        def step(b, carry):
            body(b)
            return carry

        lax.fori_loop(0, count, step, 0)


def block(b, width):
    start = b * width
    return pl.ds(start if isinstance(start, int) else pl.multiple_of(start, width), width)


def prepare(index_ref, width, size, slabs, hot_ref, mid_ref):
    shift = size.bit_length() - 1

    def body(b):
        cols = block(b, width)
        index = index_ref[:, cols]
        column = ((index >> (2 * shift)) << shift) | (index & (size - 1))
        mid = (index >> shift) & (size - 1)
        spot = lax.broadcasted_iota(jnp.int32, (slabs * size, width), 0)
        hot_ref[:, cols] = jnp.where(spot == column, 1.0, 0.0).astype(BF16)
        spot = lax.broadcasted_iota(jnp.int32, (size, width), 0)
        mid_ref[:, cols] = jnp.where(spot == mid, 1.0, 0.0).astype(BF16)

    for_blocks(index_ref.shape[1] // width, body)


def gather_rows(second, width, mid_ref, rows_ref):
    def body(b):
        cols = block(b, width)
        hot = mid_ref[:, cols]
        rows_ref[:, cols] = dot(second, jnp.concatenate([hot, hot], axis=0))

    for_blocks(mid_ref.shape[1] // width, body)


def half_picks(state_ref, p, gate, width, hot_ref, rows_ref, picked_ref, send_ref, scale):
    size = gate.shape[0] // 2
    rows = state_ref.shape[1] // 2
    slabs = rows // size
    real = state_ref[p, pl.ds(0, rows, stride=2), :]
    imag = state_ref[p, pl.ds(1, rows, stride=2), :]
    xh, xl = split(jnp.concatenate([real, imag], axis=1))
    first = dot(jnp.concatenate([xh, xl, xh], axis=1), gate, ((1,), (1,)))
    parts = [
        jnp.concatenate(
            [first[h * size : (h + 1) * size, c * size : (c + 1) * size] for h in range(slabs)], axis=1
        )
        for c in range(2)
    ]
    high, low = split(jnp.concatenate(parts, axis=0))
    picked_ref[: 2 * size, :] = high
    picked_ref[2 * size :, :] = low

    def body(b):
        cols = block(b, width)
        found = dot(picked_ref[...], hot_ref[:, cols])
        found = found[: 2 * size] + found[2 * size :]
        fr, fi = found[:size], found[size:]
        vr, vi = rows_ref[:size, cols], rows_ref[size:, cols]
        out_r = jnp.sum(vr * fr - vi * fi, axis=0, keepdims=True)
        out_i = jnp.sum(vr * fi + vi * fr, axis=0, keepdims=True)
        lanes = width // 128
        send_ref[b, p] = (
            jnp.concatenate(
                [o[:, k * 128 : (k + 1) * 128] for o in (out_r, out_i) for k in range(lanes)], axis=0
            )
            * scale
        )

    for_blocks(hot_ref.shape[1] // width, body)


def kernel(
    counts,
    left_ref,
    right_ref,
    gates_ref,
    left_index_ref,
    right_index_ref,
    out_ref,
    left_buf,
    right_buf,
    gates_buf,
    index_l,
    index_r,
    hot_l,
    hot_r,
    mid_l,
    mid_r,
    second_l,
    second_r,
    picked,
    send_l,
    send_r,
    recv_l,
    recv_r,
    load_sem,
    send_sem,
    recv_sem,
):
    row_count, col_count, sub_count = counts
    group = col_count * sub_count
    n = row_count * group
    size = gates_buf.shape[-1]
    held = left_buf.shape[0]
    slabs = left_buf.shape[1] // 2 // size
    tile_l = index_l.shape[1] // row_count
    tile_r = index_r.shape[1] // group
    r, c, s = lax.axis_index("rows"), lax.axis_index("cols"), lax.axis_index("sub")
    mine = c * sub_count + s
    me = r * group + mine

    loads = [
        pltpu.make_async_copy(src, dst, load_sem.at[i])
        for i, (src, dst) in enumerate(
            [
                (left_index_ref, index_l),
                (right_index_ref, index_r),
                (gates_ref, gates_buf),
                (left_ref, left_buf),
                (right_ref, right_buf),
            ]
        )
    ]
    for load in loads:
        load.start()

    def each_peer(act):
        if n <= 16:
            rows = [lax.rem(r + k, row_count) for k in range(row_count)]
            cols = [lax.rem(c + k, col_count) for k in range(col_count)]
            subs = [lax.rem(s + k, sub_count) for k in range(sub_count)]
            for i in reversed(range(n)):
                a, b, d = i // group, i // sub_count % col_count, i % sub_count
                if i:
                    act(rows[a], cols[b], subs[d])
        else:

            def step(offset, carry):
                d = lax.rem(me + offset, n)
                act(lax.div(d, group), lax.rem(lax.div(d, sub_count), col_count), lax.rem(d, sub_count))
                return carry

            lax.fori_loop(1, n, step, 0)

    barrier = pltpu.get_barrier_semaphore()

    def greet(a, b, d):
        where = {"rows": a, "cols": b, "sub": d}
        pl.semaphore_signal(barrier, inc=1, device_id=where, device_id_type=MESH)

    each_peer(greet)

    loads[0].wait()
    prepare(index_l, tile_l, size, slabs, hot_l, mid_l)
    loads[1].wait()
    prepare(index_r, tile_r, size, slabs, hot_r, mid_r)
    loads[2].wait()
    ur, ui = gates_buf[0, 0], gates_buf[0, 1]
    gh, gl = split(
        jnp.concatenate(
            [jnp.concatenate([ur, -ui], axis=1), jnp.concatenate([ui, ur], axis=1)], axis=0
        )
    )
    gate = jnp.concatenate([gh, gh, gl], axis=1)
    second = jnp.concatenate(
        split(jnp.concatenate([gates_buf[1, 0].T, gates_buf[1, 1].T], axis=0)), axis=1
    )
    gather_rows(second, tile_l, mid_l, second_l)
    gather_rows(second, tile_r, mid_r, second_r)

    def push(send, recv, which):
        def act(a, b, d):
            pltpu.make_async_remote_copy(
                src_ref=send.at[a if which == 0 else b * sub_count + d],
                dst_ref=recv.at[pl.ds(me * held, held)],
                send_sem=send_sem.at[which],
                recv_sem=recv_sem.at[which],
                device_id={"rows": a, "cols": b, "sub": d},
                device_id_type=MESH,
            ).start()

        each_peer(act)
        recv[pl.ds(me * held, held)] = send[r if which == 0 else mine]

    scale = 1.0 / math.sqrt(n * held)
    loads[3].wait()
    for p in range(held):
        half_picks(left_buf, p, gate, tile_l, hot_l, second_l, picked, send_l, scale)
    pl.semaphore_wait(barrier, n - 1)
    push(send_l, recv_l, 0)
    loads[4].wait()
    for p in range(held):
        half_picks(right_buf, p, gate, tile_r, hot_r, second_r, picked, send_r, 1.0)
    push(send_r, recv_r, 1)

    def take(recv):
        rows = recv.shape[1]
        flat = recv.reshape(recv.shape[0] * rows, 128)
        pieces = [flat[pl.ds(t, recv.shape[0], stride=rows), :] for t in range(rows)]
        return [jnp.concatenate(pieces[k : k + rows // 2], axis=1) for k in (0, rows // 2)]

    def await_bytes(ref, sem):
        pltpu.make_async_copy(ref, ref, sem).wait()

    others = pl.ds(0, (n - 1) * held)
    await_bytes(recv_l.at[others], recv_sem.at[0])
    lr, li = take(recv_l)
    lh, ll = split(jnp.concatenate([lr, li], axis=0))
    left = jnp.concatenate([lh, lh, ll], axis=0)
    await_bytes(recv_r.at[others], recv_sem.at[1])
    rr, ri = take(recv_r)
    rh, rl = split(
        jnp.concatenate(
            [jnp.concatenate([rr, -ri], axis=0), jnp.concatenate([ri, rr], axis=0)], axis=1
        )
    )
    right = jnp.concatenate([rh, rl, rh], axis=0)
    result = dot(left, right, ((0,), (0,)))
    out_ref[0] = result[:, :tile_r]
    out_ref[1] = result[:, tile_r:]
    await_bytes(recv_l.at[others], send_sem.at[0])
    await_bytes(recv_r.at[others], send_sem.at[1])


def per_device(counts, left_states, right_states, gates, left_index, right_index):
    row_count, col_count, sub_count = counts
    group = col_count * sub_count
    n = row_count * group
    size = gates.shape[-1]
    held = left_states.shape[0]
    nleft, nright = left_index.shape[0], right_index.shape[0]
    tile_l, tile_r = nleft // row_count, nright // group
    slab = left_states.shape[2]

    def rows_of(states):
        return states.reshape(held, 2, slab // size, size).transpose(0, 2, 1, 3).reshape(held, -1, size)

    hbm = pl.BlockSpec(memory_space=pltpu.HBM)
    rows = slab // size
    return pl.pallas_call(
        functools.partial(kernel, counts),
        out_shape=jax.ShapeDtypeStruct((2, tile_l, tile_r), F32),
        in_specs=[hbm] * 5,
        out_specs=pl.BlockSpec(memory_space=pltpu.VMEM),
        scratch_shapes=[
            pltpu.VMEM((held, 2 * rows, size), F32),
            pltpu.VMEM((held, 2 * rows, size), F32),
            pltpu.VMEM(gates.shape, F32),
            pltpu.VMEM((1, nleft), jnp.int32),
            pltpu.VMEM((1, nright), jnp.int32),
            pltpu.VMEM((rows, nleft), BF16),
            pltpu.VMEM((rows, nright), BF16),
            pltpu.VMEM((size, nleft), BF16),
            pltpu.VMEM((size, nright), BF16),
            pltpu.VMEM((2 * size, nleft), F32),
            pltpu.VMEM((2 * size, nright), F32),
            pltpu.VMEM((4 * size, rows), BF16),
            pltpu.VMEM((row_count, held, 2 * tile_l // 128, 128), F32),
            pltpu.VMEM((group, held, 2 * tile_r // 128, 128), F32),
            pltpu.VMEM((n * held, 2 * tile_l // 128, 128), F32),
            pltpu.VMEM((n * held, 2 * tile_r // 128, 128), F32),
            pltpu.SemaphoreType.DMA((5,)),
            pltpu.SemaphoreType.DMA((2,)),
            pltpu.SemaphoreType.DMA((2,)),
        ],
        compiler_params=pltpu.CompilerParams(
            collective_id=0, has_side_effects=True, vmem_limit_bytes=48 * 1024 * 1024
        ),
    )(
        *(
            pltpu.with_memory_space_constraint(x, pltpu.HBM)
            for x in (
                rows_of(left_states),
                rows_of(right_states),
                gates,
                left_index.reshape(1, nleft),
                right_index.reshape(1, nright),
            )
        )
    )


def solution(mesh):
    counts = tuple(mesh.shape[a] for a in ("rows", "cols", "sub"))
    return jax.shard_map(
        functools.partial(per_device, counts),
        mesh=mesh,
        in_specs=(
            P(("parts", "rows", "cols", "sub"), None, None),
            P(("parts", "rows", "cols", "sub"), None, None),
            P("parts", None, None, None),
            P("parts"),
            P("parts"),
        ),
        out_specs=P("parts", "rows", ("cols", "sub")),
        check_vma=False,
    )
```

time: 17 us -> 13.8 us (0.81); the launches traced: 16.7 us -> 13.7 us
  local copies, waits for them, and re-layouts: 5.2 us -> 0.8 us
  Pallas kernels: 11.4 us -> 12.8 us
    unnamed x11 -> x1, local copies, waits for them, and re-layouts: 5.2 us -> 0.8 us
    pallas_call x1, Pallas kernels: 11.4 us -> 12.8 us  [per_device(): pl.pallas_call(functools.partial(kernel, counts), out_shape=jax.ShapeDtyp...]
where the time goes in v2:
time: 13.8 us; the launch traced here: 13.7 us
  Pallas kernels  12.8 us (93%)
  local copies, waits for them, and re-layouts  0.8 us (6%)
    pallas_call x1, Pallas kernels, per_device(): pl.pallas_call(functools.partial(kernel, counts), out_shape=jax.ShapeDtyp...  12.8 us
    unnamed x1, local copies, waits for them, and re-layouts  0.8 us

profile of v2, /device:TPU:0, one launch (start us, length us, event | category | flops | bytes accessed | tf_op | source)
XLA Modules:
  0.0 13.7 jit_solution(6426162428123638528)
XLA Ops:
  0.0 12.8 %shard_map.55 = f32[2,256,256]{2,1,0:T(8,128)S(1)} custom-call(f32[1,1024,128]{2,1,0:T(8,128)} %bitcast.12, f32[1,1024,128]{2,1,0:T(8,128)} %bitcast.13, f32[2,2,128,128]{3,2,1,0:T(8,128)} %gates_ref.1, s32[1,1024]{1,0:T(1,128)} %bitcast.14, s32[1,1024]{1,0:T(1,128)} %bitcast.15), custom_call_target="tpu_custom_call" | custom-call | tf_op jit(solution)/shard_map/pallas_call | solution.py:273
  12.9 0.8 %copy.9 = f32[2,256,256]{2,1,0:T(8,128)} copy(f32[2,256,256]{2,1,0:T(8,128)S(1)} %shard_map.55) | data formatting | bytes 1048576

commit v3 on v2

--- a/solution.py
+++ b/solution.py
@@ -65,14 +65,14 @@
     for_blocks(mid_ref.shape[1] // width, body)
 
 
-def half_picks(state_ref, p, gate, width, hot_ref, rows_ref, picked_ref, send_ref, scale):
-    size = gate.shape[0] // 2
-    rows = state_ref.shape[1] // 2
+def half_picks(state_ref, gate, width, hot_ref, rows_ref, picked_ref, emit):
+    size = gate.shape[1] // 2
+    rows = state_ref.shape[0] // 2
     slabs = rows // size
-    real = state_ref[p, pl.ds(0, rows, stride=2), :]
-    imag = state_ref[p, pl.ds(1, rows, stride=2), :]
+    real = state_ref[pl.ds(0, rows, stride=2), :]
+    imag = state_ref[pl.ds(1, rows, stride=2), :]
     xh, xl = split(jnp.concatenate([real, imag], axis=1))
-    first = dot(jnp.concatenate([xh, xl, xh], axis=1), gate, ((1,), (1,)))
+    first = dot(jnp.concatenate([xh, xl, xh], axis=1), gate)
     parts = [
         jnp.concatenate(
             [first[h * size : (h + 1) * size, c * size : (c + 1) * size] for h in range(slabs)], axis=1
@@ -92,11 +92,11 @@
         out_r = jnp.sum(vr * fr - vi * fi, axis=0, keepdims=True)
         out_i = jnp.sum(vr * fi + vi * fr, axis=0, keepdims=True)
         lanes = width // 128
-        send_ref[b, p] = (
+        emit(
+            b,
             jnp.concatenate(
                 [o[:, k * 128 : (k + 1) * 128] for o in (out_r, out_i) for k in range(lanes)], axis=0
-            )
-            * scale
+            ),
         )
 
     for_blocks(hot_ref.shape[1] // width, body)
@@ -122,10 +122,8 @@
     second_l,
     second_r,
     picked,
-    send_l,
-    send_r,
-    recv_l,
-    recv_r,
+    send,
+    recv,
     load_sem,
     send_sem,
     recv_sem,
@@ -141,6 +139,9 @@
     r, c, s = lax.axis_index("rows"), lax.axis_index("cols"), lax.axis_index("sub")
     mine = c * sub_count + s
     me = r * group + mine
+    rows_l, rows_r = 2 * tile_l // 128, 2 * tile_r // 128
+    unit = rows_l + rows_r
+    slot = held * unit
 
     loads = [
         pltpu.make_async_copy(src, dst, load_sem.at[i])
@@ -149,8 +150,11 @@
                 (left_index_ref, index_l),
                 (right_index_ref, index_r),
                 (gates_ref, gates_buf),
-                (left_ref, left_buf),
-                (right_ref, right_buf),
+            ]
+            + [
+                (src.at[:, pl.ds(h * 2 * size, 2 * size)], dst.at[:, pl.ds(h * 2 * size, 2 * size)])
+                for src, dst in ((left_ref, left_buf), (right_ref, right_buf))
+                for h in range(slabs)
             ]
         )
     ]
@@ -189,70 +193,73 @@
     prepare(index_r, tile_r, size, slabs, hot_r, mid_r)
     loads[2].wait()
     ur, ui = gates_buf[0, 0], gates_buf[0, 1]
+    ur, ui = ur.T, ui.T
     gh, gl = split(
         jnp.concatenate(
-            [jnp.concatenate([ur, -ui], axis=1), jnp.concatenate([ui, ur], axis=1)], axis=0
-        )
-    )
-    gate = jnp.concatenate([gh, gh, gl], axis=1)
+            [jnp.concatenate([ur, ui], axis=1), jnp.concatenate([-ui, ur], axis=1)], axis=0
+        )
+    )
+    gate = jnp.concatenate([gh, gh, gl], axis=0)
     second = jnp.concatenate(
         split(jnp.concatenate([gates_buf[1, 0].T, gates_buf[1, 1].T], axis=0)), axis=1
     )
     gather_rows(second, tile_l, mid_l, second_l)
     gather_rows(second, tile_r, mid_r, second_r)
 
-    def push(send, recv, which):
-        def act(a, b, d):
-            pltpu.make_async_remote_copy(
-                src_ref=send.at[a if which == 0 else b * sub_count + d],
-                dst_ref=recv.at[pl.ds(me * held, held)],
-                send_sem=send_sem.at[which],
-                recv_sem=recv_sem.at[which],
-                device_id={"rows": a, "cols": b, "sub": d},
-                device_id_type=MESH,
-            ).start()
-
-        each_peer(act)
-        recv[pl.ds(me * held, held)] = send[r if which == 0 else mine]
-
     scale = 1.0 / math.sqrt(n * held)
-    loads[3].wait()
+    for load in loads[3:]:
+        load.wait()
     for p in range(held):
-        half_picks(left_buf, p, gate, tile_l, hot_l, second_l, picked, send_l, scale)
+
+        def emit_left(b, rows, p=p):
+            rows = rows * scale
+            for g in range(group):
+                send[b * group + g, p * unit : p * unit + rows_l, :] = rows
+
+        def emit_right(b, rows, p=p):
+            for a in range(row_count):
+                send[a * group + b, p * unit + rows_l : (p + 1) * unit, :] = rows
+
+        half_picks(left_buf.at[p], gate, tile_l, hot_l, second_l, picked.at[0], emit_left)
+        half_picks(right_buf.at[p], gate, tile_r, hot_r, second_r, picked.at[1], emit_right)
+
     pl.semaphore_wait(barrier, n - 1)
-    push(send_l, recv_l, 0)
-    loads[4].wait()
-    for p in range(held):
-        half_picks(right_buf, p, gate, tile_r, hot_r, second_r, picked, send_r, 1.0)
-    push(send_r, recv_r, 1)
-
-    def take(recv):
-        rows = recv.shape[1]
-        flat = recv.reshape(recv.shape[0] * rows, 128)
-        pieces = [flat[pl.ds(t, recv.shape[0], stride=rows), :] for t in range(rows)]
-        return [jnp.concatenate(pieces[k : k + rows // 2], axis=1) for k in (0, rows // 2)]
-
-    def await_bytes(ref, sem):
-        pltpu.make_async_copy(ref, ref, sem).wait()
-
-    others = pl.ds(0, (n - 1) * held)
-    await_bytes(recv_l.at[others], recv_sem.at[0])
-    lr, li = take(recv_l)
+    spot = pl.ds(pl.multiple_of(me * slot, slot), slot)
+
+    def push(a, b, d):
+        pltpu.make_async_remote_copy(
+            src_ref=send.at[a * group + b * sub_count + d],
+            dst_ref=recv.at[spot, :],
+            send_sem=send_sem,
+            recv_sem=recv_sem,
+            device_id={"rows": a, "cols": b, "sub": d},
+            device_id_type=MESH,
+        ).start()
+
+    each_peer(push)
+    recv[spot, :] = send[me]
+    others = recv.at[pl.ds(0, (n - 1) * slot), :]
+    pltpu.make_async_copy(others, others, recv_sem).wait()
+
+    def take(start, rows):
+        return jnp.concatenate(
+            [recv[pl.ds(start + t, n * held, stride=unit), :] for t in range(rows)], axis=1
+        )
+
+    lr, li = take(0, rows_l // 2), take(rows_l // 2, rows_l // 2)
+    rr, ri = take(rows_l, rows_r // 2), take(rows_l + rows_r // 2, rows_r // 2)
     lh, ll = split(jnp.concatenate([lr, li], axis=0))
-    left = jnp.concatenate([lh, lh, ll], axis=0)
-    await_bytes(recv_r.at[others], recv_sem.at[1])
-    rr, ri = take(recv_r)
     rh, rl = split(
         jnp.concatenate(
             [jnp.concatenate([rr, -ri], axis=0), jnp.concatenate([ri, rr], axis=0)], axis=1
         )
     )
+    left = jnp.concatenate([lh, lh, ll], axis=0)
     right = jnp.concatenate([rh, rl, rh], axis=0)
     result = dot(left, right, ((0,), (0,)))
     out_ref[0] = result[:, :tile_r]
     out_ref[1] = result[:, tile_r:]
-    await_bytes(recv_l.at[others], send_sem.at[0])
-    await_bytes(recv_r.at[others], send_sem.at[1])
+    pltpu.make_async_copy(others, others, send_sem).wait()
 
 
 def per_device(counts, left_states, right_states, gates, left_index, right_index):
@@ -263,6 +270,7 @@
     held = left_states.shape[0]
     nleft, nright = left_index.shape[0], right_index.shape[0]
     tile_l, tile_r = nleft // row_count, nright // group
+    unit = 2 * (tile_l + tile_r) // 128
     slab = left_states.shape[2]
 
     def rows_of(states):
@@ -287,14 +295,12 @@
             pltpu.VMEM((size, nright), BF16),
             pltpu.VMEM((2 * size, nleft), F32),
             pltpu.VMEM((2 * size, nright), F32),
-            pltpu.VMEM((4 * size, rows), BF16),
-            pltpu.VMEM((row_count, held, 2 * tile_l // 128, 128), F32),
-            pltpu.VMEM((group, held, 2 * tile_r // 128, 128), F32),
-            pltpu.VMEM((n * held, 2 * tile_l // 128, 128), F32),
-            pltpu.VMEM((n * held, 2 * tile_r // 128, 128), F32),
-            pltpu.SemaphoreType.DMA((5,)),
-            pltpu.SemaphoreType.DMA((2,)),
-            pltpu.SemaphoreType.DMA((2,)),
+            pltpu.VMEM((2, 4 * size, rows), BF16),
+            pltpu.VMEM((n, held * unit, 128), F32),
+            pltpu.VMEM((n * held * unit, 128), F32),
+            pltpu.SemaphoreType.DMA((3 + 2 * (rows // size),)),
+            pltpu.SemaphoreType.DMA,
+            pltpu.SemaphoreType.DMA,
         ],
         compiler_params=pltpu.CompilerParams(
             collective_id=0, has_side_effects=True, vmem_limit_bytes=48 * 1024 * 1024

time: 13.8 us -> 13.3 us (0.964)
  Pallas kernels: 12.8 us -> 12.3 us
    pallas_call x1, Pallas kernels: 12.8 us -> 12.3 us  [per_device(): pl.pallas_call(functools.partial(kernel, counts), out_shape=jax.ShapeDtyp...]
where the time goes in v3:
time: 13.3 us; the launch traced here: 13.1 us
  Pallas kernels  12.3 us (92%)
  local copies, waits for them, and re-layouts  0.8 us (6%)
    pallas_call x1, Pallas kernels, per_device(): pl.pallas_call(functools.partial(kernel, counts), out_shape=jax.ShapeDtyp...  12.3 us
    unnamed x1, local copies, waits for them, and re-layouts  0.8 us

profile of v3, /device:TPU:0, one launch (start us, length us, event | category | flops | bytes accessed | tf_op | source)
XLA Modules:
  0.0 13.1 jit_solution(15186498084975181910)
XLA Ops:
  0.0 12.3 %shard_map.55 = f32[2,256,256]{2,1,0:T(8,128)S(1)} custom-call(f32[1,1024,128]{2,1,0:T(8,128)} %bitcast.12, f32[1,1024,128]{2,1,0:T(8,128)} %bitcast.13, f32[2,2,128,128]{3,2,1,0:T(8,128)} %gates_ref.1, s32[1,1024]{1,0:T(1,128)} %bitcast.14, s32[1,1024]{1,0:T(1,128)} %bitcast.15), custom_call_target="tpu_custom_call" | custom-call | tf_op jit(solution)/shard_map/pallas_call | solution.py:281
  12.3 0.8 %copy.9 = f32[2,256,256]{2,1,0:T(8,128)} copy(f32[2,256,256]{2,1,0:T(8,128)S(1)} %shard_map.55) | data formatting | bytes 1048576

commit v4 on v3

--- a/solution.py
+++ b/solution.py
@@ -23,7 +23,7 @@
 
 
 def for_blocks(count, body):
-    if count <= 4:
+    if count <= 8:
         for b in range(count):
             body(b)
     else:
@@ -40,66 +40,61 @@
     return pl.ds(start if isinstance(start, int) else pl.multiple_of(start, width), width)
 
 
-def prepare(index_ref, width, size, slabs, hot_ref, mid_ref):
-    shift = size.bit_length() - 1
-
-    def body(b):
-        cols = block(b, width)
-        index = index_ref[:, cols]
-        column = ((index >> (2 * shift)) << shift) | (index & (size - 1))
-        mid = (index >> shift) & (size - 1)
-        spot = lax.broadcasted_iota(jnp.int32, (slabs * size, width), 0)
-        hot_ref[:, cols] = jnp.where(spot == column, 1.0, 0.0).astype(BF16)
-        spot = lax.broadcasted_iota(jnp.int32, (size, width), 0)
-        mid_ref[:, cols] = jnp.where(spot == mid, 1.0, 0.0).astype(BF16)
-
-    for_blocks(index_ref.shape[1] // width, body)
-
-
-def gather_rows(second, width, mid_ref, rows_ref):
-    def body(b):
-        cols = block(b, width)
-        hot = mid_ref[:, cols]
-        rows_ref[:, cols] = dot(second, jnp.concatenate([hot, hot], axis=0))
-
-    for_blocks(mid_ref.shape[1] // width, body)
-
-
-def half_picks(state_ref, gate, width, hot_ref, rows_ref, picked_ref, emit):
-    size = gate.shape[1] // 2
+def lanes(values, index):
+    spread = jnp.broadcast_to(index, (values.shape[0], index.shape[1]))
+    return jnp.take_along_axis(values, spread, axis=1, mode="promise_in_bounds")
+
+
+def apply_first(state_ref, gate, first_ref):
     rows = state_ref.shape[0] // 2
-    slabs = rows // size
     real = state_ref[pl.ds(0, rows, stride=2), :]
     imag = state_ref[pl.ds(1, rows, stride=2), :]
     xh, xl = split(jnp.concatenate([real, imag], axis=1))
-    first = dot(jnp.concatenate([xh, xl, xh], axis=1), gate)
-    parts = [
-        jnp.concatenate(
-            [first[h * size : (h + 1) * size, c * size : (c + 1) * size] for h in range(slabs)], axis=1
-        )
-        for c in range(2)
-    ]
-    high, low = split(jnp.concatenate(parts, axis=0))
-    picked_ref[: 2 * size, :] = high
-    picked_ref[2 * size :, :] = low
+    first_ref[...] = dot(jnp.concatenate([xh, xl, xh], axis=1), gate)
+
+
+def gather_rows(second, index_ref, rows_ref):
+    size = second[0].shape[0]
+    shift = size.bit_length() - 1
 
     def body(b):
-        cols = block(b, width)
-        found = dot(picked_ref[...], hot_ref[:, cols])
-        found = found[: 2 * size] + found[2 * size :]
-        fr, fi = found[:size], found[size:]
-        vr, vi = rows_ref[:size, cols], rows_ref[size:, cols]
-        out_r = jnp.sum(vr * fr - vi * fi, axis=0, keepdims=True)
-        out_i = jnp.sum(vr * fi + vi * fr, axis=0, keepdims=True)
-        lanes = width // 128
-        emit(
-            b,
-            jnp.concatenate(
-                [o[:, k * 128 : (k + 1) * 128] for o in (out_r, out_i) for k in range(lanes)], axis=0
-            ),
-        )
-
-    for_blocks(hot_ref.shape[1] // width, body)
+        cols = block(b, size)
+        mid = (index_ref[:, cols] >> shift) & (size - 1)
+        rows_ref[:size, cols] = lanes(second[0], mid)
+        rows_ref[size:, cols] = lanes(second[1], mid)
+
+    for_blocks(index_ref.shape[1] // size, body)
+
+
+def half_picks(first_ref, width, index_ref, rows_ref, emit):
+    size = first_ref.shape[1] // 2
+    shift = size.bit_length() - 1
+    slabs = first_ref.shape[0] // size
+
+    def body(b):
+        out_r, out_i = [], []
+        for k in range(width // size):
+            cols = block(b * (width // size) + k, size)
+            index = index_ref[:, cols]
+            low = index & (size - 1)
+            slab = jnp.broadcast_to(index >> (2 * shift), (size, size))
+            found = []
+            for c in range(2):
+                part = [
+                    lanes(first_ref[h * size : (h + 1) * size, c * size : (c + 1) * size], low)
+                    for h in range(slabs)
+                ]
+                value = part[0]
+                for h in range(1, slabs):
+                    value = jnp.where(slab == h, part[h], value)
+                found.append(value)
+            fr, fi = found
+            vr, vi = rows_ref[:size, cols], rows_ref[size:, cols]
+            out_r.append(jnp.sum(vr * fr - vi * fi, axis=0, keepdims=True))
+            out_i.append(jnp.sum(vr * fi + vi * fr, axis=0, keepdims=True))
+        emit(b, jnp.concatenate(out_r + out_i, axis=0))
+
+    for_blocks(index_ref.shape[1] // width, body)
 
 
 def kernel(
@@ -115,10 +110,6 @@
     gates_buf,
     index_l,
     index_r,
-    hot_l,
-    hot_r,
-    mid_l,
-    mid_r,
     second_l,
     second_r,
     picked,
@@ -188,9 +179,7 @@
     each_peer(greet)
 
     loads[0].wait()
-    prepare(index_l, tile_l, size, slabs, hot_l, mid_l)
     loads[1].wait()
-    prepare(index_r, tile_r, size, slabs, hot_r, mid_r)
     loads[2].wait()
     ur, ui = gates_buf[0, 0], gates_buf[0, 1]
     ur, ui = ur.T, ui.T
@@ -200,11 +189,9 @@
         )
     )
     gate = jnp.concatenate([gh, gh, gl], axis=0)
-    second = jnp.concatenate(
-        split(jnp.concatenate([gates_buf[1, 0].T, gates_buf[1, 1].T], axis=0)), axis=1
-    )
-    gather_rows(second, tile_l, mid_l, second_l)
-    gather_rows(second, tile_r, mid_r, second_r)
+    second = (gates_buf[1, 0].T, gates_buf[1, 1].T)
+    gather_rows(second, index_l, second_l)
+    gather_rows(second, index_r, second_r)
 
     scale = 1.0 / math.sqrt(n * held)
     for load in loads[3:]:
@@ -220,8 +207,10 @@
             for a in range(row_count):
                 send[a * group + b, p * unit + rows_l : (p + 1) * unit, :] = rows
 
-        half_picks(left_buf.at[p], gate, tile_l, hot_l, second_l, picked.at[0], emit_left)
-        half_picks(right_buf.at[p], gate, tile_r, hot_r, second_r, picked.at[1], emit_right)
+        apply_first(left_buf.at[p], gate, picked.at[0])
+        apply_first(right_buf.at[p], gate, picked.at[1])
+        half_picks(picked.at[0], tile_l, index_l, second_l, emit_left)
+        half_picks(picked.at[1], tile_r, index_r, second_r, emit_right)
 
     pl.semaphore_wait(barrier, n - 1)
     spot = pl.ds(pl.multiple_of(me * slot, slot), slot)
@@ -289,13 +278,9 @@
             pltpu.VMEM(gates.shape, F32),
             pltpu.VMEM((1, nleft), jnp.int32),
             pltpu.VMEM((1, nright), jnp.int32),
-            pltpu.VMEM((rows, nleft), BF16),
-            pltpu.VMEM((rows, nright), BF16),
-            pltpu.VMEM((size, nleft), BF16),
-            pltpu.VMEM((size, nright), BF16),
             pltpu.VMEM((2 * size, nleft), F32),
             pltpu.VMEM((2 * size, nright), F32),
-            pltpu.VMEM((2, 4 * size, rows), BF16),
+            pltpu.VMEM((2, rows, 2 * size), F32),
             pltpu.VMEM((n, held * unit, 128), F32),
             pltpu.VMEM((n * held * unit, 128), F32),
             pltpu.SemaphoreType.DMA((3 + 2 * (rows // size),)),

time: 13.3 us -> 14.4 us (1.083)
  Pallas kernels: 12.3 us -> 13.4 us
    pallas_call x1, Pallas kernels: 12.3 us -> 13.4 us  [per_device(): pl.pallas_call(functools.partial(kernel, counts), out_shape=jax.ShapeDtyp...]
where the time goes in v4:
time: 14.4 us; the launch traced here: 14.2 us
  Pallas kernels  13.4 us (93%)
  local copies, waits for them, and re-layouts  0.8 us (6%)
    pallas_call x1, Pallas kernels, per_device(): pl.pallas_call(functools.partial(kernel, counts), out_shape=jax.ShapeDtyp...  13.4 us
    unnamed x1, local copies, waits for them, and re-layouts  0.8 us

profile of v4, /device:TPU:0, one launch (start us, length us, event | category | flops | bytes accessed | tf_op | source)
XLA Modules:
  0.0 14.2 jit_solution(876425051183245306)
XLA Ops:
  0.0 13.4 %shard_map.55 = f32[2,256,256]{2,1,0:T(8,128)S(1)} custom-call(f32[1,1024,128]{2,1,0:T(8,128)} %bitcast.12, f32[1,1024,128]{2,1,0:T(8,128)} %bitcast.13, f32[2,2,128,128]{3,2,1,0:T(8,128)} %gates_ref.1, s32[1,1024]{1,0:T(1,128)} %bitcast.14, s32[1,1024]{1,0:T(1,128)} %bitcast.15), custom_call_target="tpu_custom_call" | custom-call | tf_op jit(solution)/shard_map/pallas_call | solution.py:270
  13.4 0.8 %copy.9 = f32[2,256,256]{2,1,0:T(8,128)} copy(f32[2,256,256]{2,1,0:T(8,128)S(1)} %shard_map.55) | data formatting | bytes 1048576

commit v5 on v3

--- a/solution.py
+++ b/solution.py
@@ -40,32 +40,31 @@
     return pl.ds(start if isinstance(start, int) else pl.multiple_of(start, width), width)
 
 
-def prepare(index_ref, width, size, slabs, hot_ref, mid_ref):
+def prepare(index_ref, width, size, slabs, hot_ref):
     shift = size.bit_length() - 1
 
     def body(b):
         cols = block(b, width)
         index = index_ref[:, cols]
         column = ((index >> (2 * shift)) << shift) | (index & (size - 1))
-        mid = (index >> shift) & (size - 1)
         spot = lax.broadcasted_iota(jnp.int32, (slabs * size, width), 0)
         hot_ref[:, cols] = jnp.where(spot == column, 1.0, 0.0).astype(BF16)
-        spot = lax.broadcasted_iota(jnp.int32, (size, width), 0)
-        mid_ref[:, cols] = jnp.where(spot == mid, 1.0, 0.0).astype(BF16)
 
     for_blocks(index_ref.shape[1] // width, body)
 
 
-def gather_rows(second, width, mid_ref, rows_ref):
-    def body(b):
-        cols = block(b, width)
-        hot = mid_ref[:, cols]
-        rows_ref[:, cols] = dot(second, jnp.concatenate([hot, hot], axis=0))
-
-    for_blocks(mid_ref.shape[1] // width, body)
-
-
-def half_picks(state_ref, gate, width, hot_ref, rows_ref, picked_ref, emit):
+def gather_rows(second, index):
+    size = second.shape[0]
+    shift = size.bit_length() - 1
+    pieces = []
+    for k in range(index.shape[1] // size):
+        mid = (index[:, k * size : (k + 1) * size] >> shift) & (size - 1)
+        spread = jnp.broadcast_to(mid, (size, size))
+        pieces.append(jnp.take_along_axis(second, spread, axis=1, mode="promise_in_bounds"))
+    return jnp.concatenate(pieces, axis=1)
+
+
+def half_picks(state_ref, gate, width, hot_ref, index_ref, second_ref, picked_ref, emit):
     size = gate.shape[1] // 2
     rows = state_ref.shape[0] // 2
     slabs = rows // size
@@ -88,7 +87,8 @@
         found = dot(picked_ref[...], hot_ref[:, cols])
         found = found[: 2 * size] + found[2 * size :]
         fr, fi = found[:size], found[size:]
-        vr, vi = rows_ref[:size, cols], rows_ref[size:, cols]
+        index = index_ref[:, cols]
+        vr, vi = gather_rows(second_ref[0], index), gather_rows(second_ref[1], index)
         out_r = jnp.sum(vr * fr - vi * fi, axis=0, keepdims=True)
         out_i = jnp.sum(vr * fi + vi * fr, axis=0, keepdims=True)
         lanes = width // 128
@@ -117,10 +117,7 @@
     index_r,
     hot_l,
     hot_r,
-    mid_l,
-    mid_r,
-    second_l,
-    second_r,
+    second,
     picked,
     send,
     recv,
@@ -188,9 +185,9 @@
     each_peer(greet)
 
     loads[0].wait()
-    prepare(index_l, tile_l, size, slabs, hot_l, mid_l)
+    prepare(index_l, tile_l, size, slabs, hot_l)
     loads[1].wait()
-    prepare(index_r, tile_r, size, slabs, hot_r, mid_r)
+    prepare(index_r, tile_r, size, slabs, hot_r)
     loads[2].wait()
     ur, ui = gates_buf[0, 0], gates_buf[0, 1]
     ur, ui = ur.T, ui.T
@@ -200,11 +197,8 @@
         )
     )
     gate = jnp.concatenate([gh, gh, gl], axis=0)
-    second = jnp.concatenate(
-        split(jnp.concatenate([gates_buf[1, 0].T, gates_buf[1, 1].T], axis=0)), axis=1
-    )
-    gather_rows(second, tile_l, mid_l, second_l)
-    gather_rows(second, tile_r, mid_r, second_r)
+    second[0] = gates_buf[1, 0].T
+    second[1] = gates_buf[1, 1].T
 
     scale = 1.0 / math.sqrt(n * held)
     for load in loads[3:]:
@@ -220,8 +214,8 @@
             for a in range(row_count):
                 send[a * group + b, p * unit + rows_l : (p + 1) * unit, :] = rows
 
-        half_picks(left_buf.at[p], gate, tile_l, hot_l, second_l, picked.at[0], emit_left)
-        half_picks(right_buf.at[p], gate, tile_r, hot_r, second_r, picked.at[1], emit_right)
+        half_picks(left_buf.at[p], gate, tile_l, hot_l, index_l, second, picked.at[0], emit_left)
+        half_picks(right_buf.at[p], gate, tile_r, hot_r, index_r, second, picked.at[1], emit_right)
 
     pl.semaphore_wait(barrier, n - 1)
     spot = pl.ds(pl.multiple_of(me * slot, slot), slot)
@@ -291,10 +285,7 @@
             pltpu.VMEM((1, nright), jnp.int32),
             pltpu.VMEM((rows, nleft), BF16),
             pltpu.VMEM((rows, nright), BF16),
-            pltpu.VMEM((size, nleft), BF16),
-            pltpu.VMEM((size, nright), BF16),
-            pltpu.VMEM((2 * size, nleft), F32),
-            pltpu.VMEM((2 * size, nright), F32),
+            pltpu.VMEM((2, size, size), F32),
             pltpu.VMEM((2, 4 * size, rows), BF16),
             pltpu.VMEM((n, held * unit, 128), F32),
             pltpu.VMEM((n * held * unit, 128), F32),

time: 13.3 us -> 12.7 us (0.955)
  Pallas kernels: 12.3 us -> 11.7 us
    pallas_call x1, Pallas kernels: 12.3 us -> 11.7 us  [per_device(): pl.pallas_call(functools.partial(kernel, counts), out_shape=jax.ShapeDtyp...]
where the time goes in v5:
time: 12.7 us; the launch traced here: 12.5 us
  Pallas kernels  11.7 us (92%)
  local copies, waits for them, and re-layouts  0.8 us (6%)
    pallas_call x1, Pallas kernels, per_device(): pl.pallas_call(functools.partial(kernel, counts), out_shape=jax.ShapeDtyp...  11.7 us
    unnamed x1, local copies, waits for them, and re-layouts  0.8 us

profile of v5, /device:TPU:0, one launch (start us, length us, event | category | flops | bytes accessed | tf_op | source)
XLA Modules:
  0.0 12.5 jit_solution(5569228212822951789)
XLA Ops:
  0.0 11.7 %shard_map.55 = f32[2,256,256]{2,1,0:T(8,128)S(1)} custom-call(f32[1,1024,128]{2,1,0:T(8,128)} %bitcast.12, f32[1,1024,128]{2,1,0:T(8,128)} %bitcast.13, f32[2,2,128,128]{3,2,1,0:T(8,128)} %gates_ref.1, s32[1,1024]{1,0:T(1,128)} %bitcast.14, s32[1,1024]{1,0:T(1,128)} %bitcast.15), custom_call_target="tpu_custom_call" | custom-call | tf_op jit(solution)/shard_map/pallas_call | solution.py:275
  11.7 0.8 %copy.9 = f32[2,256,256]{2,1,0:T(8,128)} copy(f32[2,256,256]{2,1,0:T(8,128)S(1)} %shard_map.55) | data formatting | bytes 1048576
